TPU v7x, 128 devices: a whole 4x4x4 slice. The times are simulated.
128 devices in a mesh: pipe: 2 (over z_hi), dp: 64 (over y, z_lo, x, core).
Axes of the slice: x: 4, y: 4, z: 4 (z_hi: 2, z_lo: 2; z = z_hi * 2 + z_lo), core: 2. Of those that a mesh axis runs over, the one named last changes fastest.
Arguments:
- video: bfloat16 [2, 64, 1088, 512], P(None, 'dp'), may hold values from -6 to 6
- cot_h: bfloat16 [2, 64, 1088, 512], P(None, 'dp'), may hold values from -6 to 6
- cot_q: bfloat16 [2, 64, 8, 1088], P(None, 'dp'), may hold values from -6 to 6
- frames: int32 [2, 64], P(None, 'dp'), may hold values from 5 to 17, as said below
- codes: int32 [2, 64, 1088], P(None, 'dp'), may hold values from 0 to 8191
- w_attn: bfloat16 [2, 512, 2048], P('pipe')
- w_up: bfloat16 [2, 512, 2048], P('pipe'), may hold values from -0.25 to 0.25
- w_down: bfloat16 [2, 2048, 512], P('pipe'), may hold values from -0.125 to 0.125
- gains: float32 [2, 2, 512], P('pipe'), may hold values from 0.5 to 1.5
- proj: bfloat16 [512, 8], P(('pipe', 'dp')), may hold values from -0.25 to 0.25
- codebook: bfloat16 [8, 8192], P(None, ('pipe', 'dp')), may hold values from -5 to 5
- ema_attn: float32 [2, 512, 2048], P('pipe', 'dp'), may hold values from -0.25 to 0.25
- ema_up: float32 [2, 512, 2048], P('pipe', 'dp'), may hold values from -0.25 to 0.25
- ema_down: float32 [2, 2048, 512], P('pipe', 'dp'), may hold values from -0.125 to 0.125
- ema_gains: float32 [2, 2, 512], P('pipe', None, 'dp'), may hold values from 0.5 to 1.5
- ema_proj: float32 [512, 8], P(('pipe', 'dp')), may hold values from -0.25 to 0.25
- ema_code: float32 [8, 8192], P(None, ('pipe', 'dp')), may hold values from -5 to 5
- decay: float32 [3], replicated, may hold values from 0.5 to 0.95
Outputs:
- acts: bfloat16 [2, 2, 64, 1088, 512], P('pipe', None, 'dp')
- grad_in: bfloat16 [2, 2, 64, 1088, 512], P('pipe', None, 'dp')
- g_attn: float32 [2, 512, 2048], P('pipe', 'dp')
- g_up: float32 [2, 512, 2048], P('pipe', 'dp')
- g_down: float32 [2, 2048, 512], P('pipe', 'dp')
- g_gains: float32 [2, 2, 512], P('pipe', None, 'dp')
- g_proj: float32 [512, 8], P(('pipe', 'dp'))
- g_code: float32 [8, 8192], P(None, ('pipe', 'dp'))
- new_attn: float32 [2, 512, 2048], P('pipe', 'dp')
- new_up: float32 [2, 512, 2048], P('pipe', 'dp')
- new_down: float32 [2, 2048, 512], P('pipe', 'dp')
- new_gains: float32 [2, 2, 512], P('pipe', None, 'dp')
- new_proj: float32 [512, 8], P(('pipe', 'dp'))
- new_code: float32 [8, 8192], P(None, ('pipe', 'dp'))
Inputs may be any that keep to these rules, and one draw needn't show every extreme that they name: `frames`: each count is 5, 9 or 17, and 17 occurs in every draw.
All inputs are finite; a program needn't handle non-finite values.
Results may differ from a plain program's by a relative error of at most 0.02.
Values may be sent and summed in bfloat16 or wider, within the bound.
A program may use at most 512 MiB of HBM per device.

v0:
```python
import jax
import jax.numpy as jnp
from jax import lax
from jax.sharding import PartitionSpec as P

D = 512
HEADS = 8
HEAD_DIM = 64
FF = 2048
CODES = 8192
CODE_DIM = 8
PATCHES = 64
FRAMES = 17
SEQ = 1088


EPSILON = 1e-05
BETA = 0.25
LEARN_RATE = 0.0001
MASKED = -1e30


def from_behind(block, axis, distance):
    devices = range(lax.axis_size(axis))
    route = [(i - distance, i) for i in devices if i - distance in devices]
    return lax.ppermute(block, axis, route)


def layer_norm(value, gain):
    center = jnp.mean(value, axis=-1, keepdims=True)
    centred = value - center
    spread = jnp.mean(centred * centred, axis=-1, keepdims=True)
    return centred * lax.rsqrt(spread + EPSILON) * gain


def spatial_groups(tokens):
    return tokens.reshape((tokens.shape[0] * FRAMES, PATCHES) + tokens.shape[2:])


def spatial_tokens(grouped, videos):
    return grouped.reshape((videos, FRAMES * PATCHES) + grouped.shape[2:])


def spatial_allowed():
    return jnp.ones((1, 1, PATCHES, PATCHES), jnp.bool_)


def attend_forward(grouped, allowed):
    query, keys, values = (grouped[:, :, 0], grouped[:, :, 1], grouped[:, :, 2])
    scores = jnp.einsum(
        "glhe,gmhe->ghlm", query, keys, preferred_element_type=jnp.float32
    ) * HEAD_DIM ** (-0.5)
    scores = jnp.where(allowed, scores, MASKED)
    highest = jnp.max(scores, axis=-1, keepdims=True)
    logsum = highest + jnp.log(jnp.sum(jnp.exp(scores - highest), axis=-1, keepdims=True))
    probs = jnp.exp(scores - logsum).astype(jnp.bfloat16)
    context = jnp.einsum("ghlm,gmhe->glhe", probs, values, preferred_element_type=jnp.float32)
    return (context.astype(jnp.bfloat16), jnp.swapaxes(logsum[..., 0], 1, 2))


def attend_backward(grouped, allowed, logsum, d_context):
    query, keys, values = (grouped[:, :, 0], grouped[:, :, 1], grouped[:, :, 2])
    scores = jnp.einsum(
        "glhe,gmhe->ghlm", query, keys, preferred_element_type=jnp.float32
    ) * HEAD_DIM ** (-0.5)
    scores = jnp.where(allowed, scores, MASKED)
    probs = jnp.exp(scores - jnp.swapaxes(logsum, 1, 2)[..., None])
    d_values = jnp.einsum(
        "ghlm,glhe->gmhe", probs.astype(jnp.bfloat16), d_context, preferred_element_type=jnp.float32
    )
    d_probs = jnp.einsum("glhe,gmhe->ghlm", d_context, values, preferred_element_type=jnp.float32)
    d_scores = probs * (d_probs - jnp.sum(d_probs * probs, axis=-1, keepdims=True))
    d_low = d_scores.astype(jnp.bfloat16)
    d_query = jnp.einsum(
        "ghlm,gmhe->glhe", d_low, keys, preferred_element_type=jnp.float32
    ) * HEAD_DIM ** (-0.5)
    d_keys = jnp.einsum(
        "ghlm,glhe->gmhe", d_low, query, preferred_element_type=jnp.float32
    ) * HEAD_DIM ** (-0.5)
    return jnp.stack([d_query, d_keys, d_values], axis=2)


def spatial_forward(mixed, frame_count):
    videos = mixed.shape[0]
    grouped = spatial_groups(mixed.reshape(videos, SEQ, 3, HEADS, HEAD_DIM))
    context, logsum = attend_forward(grouped, spatial_allowed())
    return (spatial_tokens(context, videos).reshape(videos, SEQ, D), spatial_tokens(logsum, videos))


def spatial_backward(mixed, logsum, d_context, frame_count):
    videos = mixed.shape[0]
    grouped = spatial_groups(mixed.reshape(videos, SEQ, 3, HEADS, HEAD_DIM))
    d_heads = spatial_groups(d_context.reshape(videos, SEQ, HEADS, HEAD_DIM))
    d_grouped = attend_backward(grouped, spatial_allowed(), spatial_groups(logsum), d_heads)
    return spatial_tokens(d_grouped, videos).reshape(videos, SEQ, 3 * D)


def to_lanes(tokens, parts):
    videos = tokens.shape[0]
    shaped = tokens.reshape(videos, FRAMES, PATCHES, parts, HEADS, HEAD_DIM)
    shaped = jnp.transpose(shaped, (0, 3, 1, 5, 4, 2))
    return shaped.reshape(videos, parts, FRAMES, HEAD_DIM, HEADS * PATCHES)


def from_lanes(lanes):
    videos, parts = (lanes.shape[0], lanes.shape[1])
    shaped = lanes.reshape(videos, parts, FRAMES, HEAD_DIM, HEADS, PATCHES)
    shaped = jnp.transpose(shaped, (0, 2, 5, 1, 4, 3))
    return shaped.reshape(videos, SEQ, parts * HEADS * HEAD_DIM)


def lane_scores(queries, key_lanes, frame_count):
    scores = jnp.sum(
        queries.astype(jnp.float32)[:, :, None] * key_lanes.astype(jnp.float32)[:, None], axis=3
    ) * HEAD_DIM ** (-0.5)
    frame_ids = jnp.arange(FRAMES)
    allowed = (frame_ids[None, None, :] <= frame_ids[None, :, None]) & (
        frame_ids[None, None, :] < frame_count[:, None, None]
    )
    return jnp.where(allowed[..., None], scores, MASKED)


def temporal_forward(mixed, frame_count):
    videos = mixed.shape[0]
    lanes = to_lanes(mixed, 3)
    queries, key_lanes, value_lanes = (lanes[:, 0], lanes[:, 1], lanes[:, 2])
    scores = lane_scores(queries, key_lanes, frame_count)
    highest = jnp.max(scores, axis=2, keepdims=True)
    logsum = highest + jnp.log(jnp.sum(jnp.exp(scores - highest), axis=2, keepdims=True))
    probs = jnp.exp(scores - logsum).astype(jnp.bfloat16)
    context = jnp.sum(
        probs.astype(jnp.float32)[:, :, :, None] * value_lanes.astype(jnp.float32)[:, None], axis=2
    )
    context_tokens = from_lanes(context.astype(jnp.bfloat16)[:, None])
    shaped = jnp.transpose(logsum.reshape(videos, FRAMES, HEADS, PATCHES), (0, 1, 3, 2))
    return (context_tokens, shaped.reshape(videos, SEQ, HEADS))


def temporal_backward(mixed, logsum, d_context, frame_count):
    videos = mixed.shape[0]
    lanes = to_lanes(mixed, 3)
    queries, key_lanes, value_lanes = (lanes[:, 0], lanes[:, 1], lanes[:, 2])
    lane_logsum = jnp.transpose(
        logsum.reshape(videos, FRAMES, PATCHES, HEADS), (0, 1, 3, 2)
    ).reshape(videos, FRAMES, 1, HEADS * PATCHES)
    d_lanes = to_lanes(d_context, 1)[:, 0].astype(jnp.float32)
    scores = lane_scores(queries, key_lanes, frame_count)
    probs = jnp.exp(scores - lane_logsum)
    probs_low = probs.astype(jnp.bfloat16).astype(jnp.float32)
    d_values = jnp.sum(probs_low[:, :, :, None] * d_lanes[:, :, None], axis=1)
    d_probs = jnp.sum(d_lanes[:, :, None] * value_lanes.astype(jnp.float32)[:, None], axis=3)
    d_scores = probs * (d_probs - jnp.sum(d_probs * probs, axis=2, keepdims=True))
    d_low = d_scores.astype(jnp.bfloat16).astype(jnp.float32)
    d_query = jnp.sum(
        d_low[:, :, :, None] * key_lanes.astype(jnp.float32)[:, None], axis=2
    ) * HEAD_DIM ** (-0.5)
    d_keys = jnp.sum(
        d_low[:, :, :, None] * queries.astype(jnp.float32)[:, :, None], axis=1
    ) * HEAD_DIM ** (-0.5)
    return from_lanes(jnp.stack([d_query, d_keys, d_values], axis=1))


def block_forward(weights, inputs, frame_count, first):
    weight_attn, weight_up, weight_down, gain_pair = weights
    videos = inputs.shape[0]
    flat = inputs.reshape(-1, D).astype(jnp.float32)
    normed = layer_norm(flat, gain_pair[0]).astype(jnp.bfloat16)
    mixed = jnp.dot(normed, weight_attn[:, : 3 * D], preferred_element_type=jnp.float32).astype(
        jnp.bfloat16
    )
    mixed = mixed.reshape(videos, SEQ, 3 * D)
    context, logsum = lax.cond(first, spatial_forward, temporal_forward, mixed, frame_count)
    middle = flat + jnp.dot(
        context.reshape(-1, D), weight_attn[:, 3 * D :], preferred_element_type=jnp.float32
    )
    normed_two = layer_norm(middle, gain_pair[1]).astype(jnp.bfloat16)
    hidden_pre = jnp.dot(normed_two, weight_up, preferred_element_type=jnp.float32)
    activated = jax.nn.gelu(hidden_pre).astype(jnp.bfloat16)
    output = middle + jnp.dot(activated, weight_down, preferred_element_type=jnp.float32)
    return (
        output.astype(jnp.bfloat16).reshape(videos, SEQ, D),
        (mixed, context, logsum, middle, hidden_pre),
    )


def block_backward(weights, inputs, saved, frame_count, first, d_out):
    weight_attn, weight_up, weight_down, gain_pair = weights
    mixed, context, logsum, middle, hidden_pre = saved
    videos = inputs.shape[0]
    flat = inputs.reshape(-1, D).astype(jnp.float32)
    d_two = d_out.astype(jnp.bfloat16)
    normed_two, norm_two_back = jax.vjp(layer_norm, middle, gain_pair[1])
    activated, gelu_back = jax.vjp(jax.nn.gelu, hidden_pre)
    grad_down = jnp.dot(activated.astype(jnp.bfloat16).T, d_two, preferred_element_type=jnp.float32)
    d_activated = jnp.dot(d_two, weight_down.T, preferred_element_type=jnp.float32)
    d_hidden = gelu_back(d_activated)[0].astype(jnp.bfloat16)
    grad_up = jnp.dot(
        normed_two.astype(jnp.bfloat16).T, d_hidden, preferred_element_type=jnp.float32
    )
    d_normed_two = jnp.dot(d_hidden, weight_up.T, preferred_element_type=jnp.float32)
    d_middle_norm, grad_gain_two = norm_two_back(d_normed_two)
    d_middle = d_out + d_middle_norm
    d_branch = d_middle.astype(jnp.bfloat16)
    grad_out = jnp.dot(context.reshape(-1, D).T, d_branch, preferred_element_type=jnp.float32)
    d_context = jnp.dot(
        d_branch, weight_attn[:, 3 * D :].T, preferred_element_type=jnp.float32
    ).astype(jnp.bfloat16)
    d_context = d_context.reshape(videos, SEQ, D)
    d_mixed = lax.cond(
        first, spatial_backward, temporal_backward, mixed, logsum, d_context, frame_count
    )
    d_mixed = d_mixed.reshape(-1, 3 * D).astype(jnp.bfloat16)
    normed, norm_back = jax.vjp(layer_norm, flat, gain_pair[0])
    grad_mix = jnp.dot(normed.astype(jnp.bfloat16).T, d_mixed, preferred_element_type=jnp.float32)
    d_normed = jnp.dot(d_mixed, weight_attn[:, : 3 * D].T, preferred_element_type=jnp.float32)
    d_flat, grad_gain_one = norm_back(d_normed)
    d_input = (d_middle + d_flat).astype(jnp.bfloat16).reshape(videos, SEQ, D)
    grads = (
        jnp.concatenate([grad_mix, grad_out], axis=1),
        grad_up,
        grad_down,
        jnp.stack([grad_gain_one, grad_gain_two]),
    )
    return (d_input, grads)


def valid_mask(frame_count):
    return (jnp.arange(SEQ)[None, :] // PATCHES < frame_count[:, None]).astype(jnp.float32)


def average(ema, weight, grad, rate):
    return rate * ema + (1.0 - rate) * (weight - LEARN_RATE * grad)


def per_device(
    video,
    cot_h,
    cot_q,
    frames,
    codes,
    w_attn,
    w_up,
    w_down,
    gains,
    proj,
    codebook,
    ema_attn,
    ema_up,
    ema_down,
    ema_gains,
    ema_proj,
    ema_code,
    decay,
):
    segment = lax.axis_index("pipe")
    first = segment == 0
    micro = video.shape[0]
    videos = video.shape[1]
    weights = (w_attn[0], w_up[0], w_down[0], gains[0])
    proj_all, code_all = (
        lax.all_gather(proj, ("pipe", "dp"), axis=0, tiled=True),
        lax.all_gather(codebook, ("pipe", "dp"), axis=1, tiled=True),
    )
    slots = micro + 2
    row_count = videos * SEQ

    def empty_saved():
        return (
            jnp.zeros((videos, SEQ, 3 * D), jnp.bfloat16),
            jnp.zeros((videos, SEQ, D), jnp.bfloat16),
            jnp.zeros((videos, SEQ, HEADS), jnp.float32),
            jnp.zeros((row_count, D), jnp.float32),
            jnp.zeros((row_count, FF), jnp.float32),
        )

    def empty_grads():
        return jax.tree.map(lambda w: jnp.zeros(w.shape, jnp.float32), weights)

    def empty_quant():
        return (jnp.zeros((D, CODE_DIM), jnp.float32), jnp.zeros((CODE_DIM, CODES), jnp.float32))

    def run_forward(inputs, frame_count):
        return block_forward(weights, inputs, frame_count, first)

    def skip_forward(inputs, frame_count):
        return (jnp.zeros_like(inputs), empty_saved())

    store_inputs = jnp.zeros((slots,) + video.shape[1:], jnp.bfloat16)
    store_outputs = jnp.zeros((slots,) + video.shape[1:], jnp.bfloat16)
    store_saved = jax.tree.map(lambda a: jnp.zeros((slots,) + a.shape, a.dtype), empty_saved())
    received = jnp.zeros_like(video[0])
    for tick in range(micro + 1):
        own = video[min(tick, micro - 1)]
        inputs = jnp.where(first, own, received)
        active = jnp.where(first, tick < micro, tick >= 1)
        index = jnp.clip(tick - segment, 0, micro - 1)
        frame_count = lax.dynamic_index_in_dim(frames, index, 0, keepdims=False)
        output, saved = lax.cond(active, run_forward, skip_forward, inputs, frame_count)
        which = tick - segment + 1
        store_inputs = lax.dynamic_update_index_in_dim(store_inputs, inputs, which, 0)
        store_outputs = lax.dynamic_update_index_in_dim(store_outputs, output, which, 0)
        store_saved = jax.tree.map(
            lambda buffer, value: lax.dynamic_update_index_in_dim(buffer, value, which, 0),
            store_saved,
            saved,
        )
        if tick < micro:
            received = from_behind(output, "pipe", 1)

    def from_next(out_low, code_now, cot_h_now, cot_q_now, valid, returned):
        return (returned.reshape(-1, D).astype(jnp.float32), empty_quant())

    def from_loss(out_low, code_now, cot_h_now, cot_q_now, valid, returned):
        rows = out_low.reshape(-1, D)
        mask = valid.reshape(-1, 1)
        latent = jnp.dot(rows, proj_all, preferred_element_type=jnp.float32)
        onehot_cols = (jnp.arange(CODES)[:, None] == code_now.reshape(-1)[None, :]).astype(
            jnp.bfloat16
        )
        chosen = jnp.dot(code_all, onehot_cols, preferred_element_type=jnp.float32).T
        cot_codes = jnp.swapaxes(cot_q_now, 1, 2).reshape(-1, CODE_DIM).astype(jnp.float32)
        d_latent = (cot_codes * mask + 2.0 * BETA * mask * (latent - chosen)).astype(jnp.bfloat16)
        d_chosen = (2.0 * mask * (chosen - latent)).astype(jnp.bfloat16)
        grad_proj = jnp.dot(rows.T, d_latent, preferred_element_type=jnp.float32)
        grad_code = lax.dot_general(
            d_chosen.T, onehot_cols, (((1,), (1,)), ((), ())), preferred_element_type=jnp.float32
        )
        d_rows = jnp.dot(d_latent, proj_all.T, preferred_element_type=jnp.float32)
        d_out = cot_h_now.reshape(-1, D).astype(jnp.float32) * mask + d_rows
        return (d_out, (grad_proj, grad_code))

    def run_backward(inputs, saved, out_low, frame_count, code_now, cot_h_now, cot_q_now, returned):
        valid = valid_mask(frame_count)
        d_out, quant_terms = lax.cond(
            first, from_next, from_loss, out_low, code_now, cot_h_now, cot_q_now, valid, returned
        )
        d_input, grads = block_backward(weights, inputs, saved, frame_count, first, d_out)
        return (d_input, grads, quant_terms)

    def skip_backward(
        inputs, saved, out_low, frame_count, code_now, cot_h_now, cot_q_now, returned
    ):
        return (jnp.zeros_like(inputs), empty_grads(), empty_quant())

    summed = empty_grads()
    shards = None
    quant_summed = empty_quant()
    store_back = jnp.zeros((slots,) + video.shape[1:], jnp.bfloat16)
    returned = jnp.zeros_like(video[0])
    for tick in range(micro + 1):
        index = jnp.clip(tick - 1 + segment, 0, micro - 1)
        slot = tick + segment
        active = jnp.where(first, tick >= 1, tick < micro)
        inputs = lax.dynamic_index_in_dim(store_inputs, slot, 0, keepdims=False)
        out_low = lax.dynamic_index_in_dim(store_outputs, slot, 0, keepdims=False)
        saved = jax.tree.map(
            lambda buffer: lax.dynamic_index_in_dim(buffer, slot, 0, keepdims=False), store_saved
        )
        frame_count = lax.dynamic_index_in_dim(frames, index, 0, keepdims=False)
        code_now = lax.dynamic_index_in_dim(codes, index, 0, keepdims=False)
        cot_h_now = lax.dynamic_index_in_dim(cot_h, index, 0, keepdims=False)
        cot_q_now = lax.dynamic_index_in_dim(cot_q, index, 0, keepdims=False)
        d_input, grads, quant_terms = lax.cond(
            active,
            run_backward,
            skip_backward,
            inputs,
            saved,
            out_low,
            frame_count,
            code_now,
            cot_h_now,
            cot_q_now,
            returned,
        )
        store_back = lax.dynamic_update_index_in_dim(store_back, d_input, slot, 0)
        quant_summed = jax.tree.map(lambda a, b: a + b, quant_summed, quant_terms)
        if tick < micro:
            returned = from_behind(d_input, "pipe", -1)
        summed = jax.tree.map(lambda a, b: a + b, summed, grads)
    shards = (
        lax.psum_scatter(summed[0][None], "dp", scatter_dimension=1, tiled=True),
        lax.psum_scatter(summed[1][None], "dp", scatter_dimension=1, tiled=True),
        lax.psum_scatter(summed[2][None], "dp", scatter_dimension=1, tiled=True),
        lax.psum_scatter(summed[3][None], "dp", scatter_dimension=2, tiled=True),
    )
    g_attn, g_up, g_down, g_gains = shards
    g_proj, g_code = (
        lax.psum_scatter(quant_summed[0], ("pipe", "dp"), scatter_dimension=0, tiled=True),
        lax.psum_scatter(quant_summed[1], ("pipe", "dp"), scatter_dimension=1, tiled=True),
    )
    valid_all = (jnp.arange(SEQ)[None, None, :] // PATCHES < frames[:, :, None]).astype(
        jnp.float32
    )[..., None]
    acts = (store_outputs[1 : micro + 1].astype(jnp.float32) * valid_all).astype(jnp.bfloat16)[None]
    grad_in = store_back[1 : micro + 1][None]
    lane = lax.axis_index("dp")
    parts = lax.axis_size("dp")

    def own_rows(weight, axis):
        size = weight.shape[axis] // parts
        return lax.dynamic_slice_in_dim(weight, lane * size, size, axis).astype(jnp.float32)

    rate = lax.dynamic_index_in_dim(decay, segment, 0, keepdims=False)
    new_attn = average(ema_attn, own_rows(w_attn, 1), g_attn, rate)
    new_up = average(ema_up, own_rows(w_up, 1), g_up, rate)
    new_down = average(ema_down, own_rows(w_down, 1), g_down, rate)
    new_gains = average(ema_gains, own_rows(gains, 2), g_gains, rate)
    new_proj = average(ema_proj, proj.astype(jnp.float32), g_proj, decay[2])
    new_code = average(ema_code, codebook.astype(jnp.float32), g_code, decay[2])
    return (
        acts,
        grad_in,
        g_attn,
        g_up,
        g_down,
        g_gains,
        g_proj,
        g_code,
        new_attn,
        new_up,
        new_down,
        new_gains,
        new_proj,
        new_code,
    )


def solution(mesh):
    placed = (
        P(None, "dp", None, None),
        P(None, "dp", None, None),
        P(None, "dp", None, None),
        P(None, "dp"),
        P(None, "dp", None),
        P("pipe", None, None),
        P("pipe", None, None),
        P("pipe", None, None),
        P("pipe", None, None),
        P(("pipe", "dp"), None),
        P(None, ("pipe", "dp")),
        P("pipe", "dp", None),
        P("pipe", "dp", None),
        P("pipe", "dp", None),
        P("pipe", None, "dp"),
        P(("pipe", "dp"), None),
        P(None, ("pipe", "dp")),
        P(),
    )
    return jax.shard_map(
        per_device,
        mesh=mesh,
        in_specs=placed,
        out_specs=(
            P("pipe", None, "dp", None, None),
            P("pipe", None, "dp", None, None),
            P("pipe", "dp", None),
            P("pipe", "dp", None),
            P("pipe", "dp", None),
            P("pipe", None, "dp"),
            P(("pipe", "dp"), None),
            P(None, ("pipe", "dp")),
            P("pipe", "dp", None),
            P("pipe", "dp", None),
            P("pipe", "dp", None),
            P("pipe", None, "dp"),
            P(("pipe", "dp"), None),
            P(None, ("pipe", "dp")),
        ),
        check_vma=False,
    )
```

profile of v0, /device:TPU:0, one launch (start us, length us, event | category | flops | bytes accessed | tf_op | source)
XLA Modules:
  0.0 2836.9 jit_solution(2073471978210743783)
XLA Ops:
  11.3 56.9 %conditional.13 = (bf16[1,1088,512]{2,1,0:T(8,128)(2,1)}, bf16[1,1,1088,512]{3,2,1,0:T(8,128)(2,1)}, bf16[1,1,1088,1536]{3,2,1,0:T(8,128)(2,1)}, bf16[1,1,1088,5...) conditional(s32[]{:T(128)} %convert_element_type.981, ...), branch_computations={%region_0.1_spmd, %region_1.14_spmd} | conditional | flops 7029483008 | bytes 135512096 | solution.py:298
  17.7 29.5 %conditional = (bf16[1088,512]{1,0:T(8,128)(2,1)}, bf16[1,1,1088,512]{3,2,1,0:T(8,128)(2,1)}, f32[1,1,1088,8]{2,3,1,0:T(8,128)S(1)}) conditional(s32[]{:T(128)} %convert_element_type.826, (s32[]{:T(128)}, s32[2,1]{0,1:T(1,128)S(1)}, bf16[1088,1536]{1,0:T(8,128)(2,1)}) %tuple.167, bf16[1088,1536]{1,0:T(8,128)(2,1)} %convolution_convert_fusion), branch_computations={%region_4.8_spmd, %region_9.11_spmd} | conditional | flops 147611136 | bytes 50797808 | solution.py:172
  93.9 172.3 %all-gather.1 = bf16[128,64,8]{1,2,0:T(8,128)(2,1)S(1)} all-gather(bf16[1,64,8]{1,2,0:T(8,128)(2,1)S(1)} %bitcast.938), channel_id=1, replica_groups=mesh['pipe'=2,'dp'=64] {'pipe','dp'}, dimensions={0}, use_global_device_ids=true | all-gather | bytes 132096 | tf_op jit(solution)/shard_map/all_gather | solution.py:262
  267.2 179.1 %all-gather = bf16[128,4,8]{2,1,0:T(4,128)(2,1)} all-gather(bf16[1,4,8]{2,1,0:T(4,128)(2,1)S(1)} %bitcast.942), channel_id=1, replica_groups=mesh['pipe'=2,'dp'=64] {'pipe','dp'}, dimensions={0}, use_global_device_ids=true | all-gather | bytes 8256 | tf_op jit(solution)/shard_map/all_gather | solution.py:261
  447.6 11.9 broadcast_in_dim.477
  476.1 29.5 %conditional.14 = (bf16[1088,512]{1,0:T(8,128)(2,1)}, bf16[1,1,1088,512]{3,2,1,0:T(8,128)(2,1)}, f32[1,1,1088,8]{2,3,1,0:T(8,128)S(1)}) conditional(s32[]{:T(128)} %convert_element_type.981, (s32[]{:T(128)}, s32[2,1]{0,1:T(1,128)S(1)}, bf16[1088,1536]{1,0:T(8,128)(2,1)}) %tuple.413, bf16[1088,1536]{1,0:T(8,128)(2,1)} %get-tuple-element.1930), branch_computations={%region_16.21_spmd, %region_21.24_spmd} | conditional | flops 147611136 | bytes 50797792 | solution.py:172
  519.5 12.0 collective-permute-start.1
  534.9 20.9 collective-permute-done.1
  557.1 13.9 conditional.15
  596.3 22.5 conditional.16
  631.8 299.4 %collective-permute-done.2 = bf16[1,1088,512]{2,1,0:T(8,128)(2,1)S(1)} collective-permute-done((bf16[1,1088,512]{2,1,0:T(8,128)(2,1)}, bf16[1,1088,512]{2,1,0:T(8,128)(2,1)S(1)}, u32[]{:S(2)}, u32[]{:S(2)}) %collective-permute-start.2) | collective-permute-done | bytes 1114144 | tf_op jit(solution)/shard_map/ppermute | solution.py:26
  959.0 66.7 %conditional.18 = (bf16[1,1088,1536]{2,1,0:T(8,128)(2,1)}) conditional(s32[]{:T(128)} %convert_element_type.981, (s32[1,1]{1,0:T(1,128)}, bf16[1,1088,1536]{2,1,0:T(8,128)(2,1)}, f32[1,1088,8]{1,2,0:T(8,128)S(1)}, bf16[1088,512]{1,0:T(8,128)(2,1)}) %tuple.392, (bf16[1,1088,1536]{2,1,0:T(8,128)(2,1)}, f32[1,1088,8]{1,2,0:T(8,128)S(1)}, ...), branch_computations={%region_69.76_spmd, %region_76.78_spmd} | conditional | flops 368762368 | bytes 118131648 | solution.py:209
  1005.8 10.2 copy.793
  1046.4 94.5 %collective-permute-done.3 = bf16[1,1088,512]{2,1,0:T(8,128)(2,1)} collective-permute-done((bf16[1,1088,512]{2,1,0:T(8,128)(2,1)}, bf16[1,1088,512]{2,1,0:T(8,128)(2,1)}, u32[]{:S(2)}, u32[]{:S(2)}) %collective-permute-start.3) | collective-permute-done | bytes 1114144 | tf_op jit(solution)/shard_map/ppermute | solution.py:26
  1140.9 144.9 %conditional.19 = (f32[512,2048]{1,0:T(8,128)}, f32[512,2048]{1,0:T(8,128)}, f32[2048,512]{1,0:T(8,128)}, f32[2,512]{1,0:T(2,128)S(1)}, f32[512,8]{0,1:T(8,128)S...) conditional(s32[]{:T(128)} %convert_element_type.981, () %tuple.217, ...), branch_computations={%region_82.83_spmd, %region_83.105_spmd} | conditional | flops 14491284480 | bytes 315253856 | solution.py:363
  1155.6 10.2 fusion.310
  1184.0 66.7 %conditional.5 = (bf16[1,1088,1536]{2,1,0:T(8,128)(2,1)}) conditional(s32[]{:T(128)} %convert_element_type.941, (s32[1,1]{1,0:T(1,128)}, bf16[1,1088,1536]{2,1,0:T(8,128)(2,1)}, f32[1,1088,8]{1,2,0:T(8,128)S(1)}, bf16[1088,512]{1,0:T(8,128)(2,1)}) %tuple.190, (bf16[1,1088,1536]{2,1,0:T(8,128)(2,1)}, f32[1,1088,8]{1,2,0:T(8,128)S(1)}, ...), branch_computations={%region_92.98_spmd, %region_99.100_spmd} | conditional | flops 368762368 | bytes 118131648 | solution.py:209
  1230.6 10.2 copy.808
  1335.5 170.5 %all-reduce = f32[1,2,512]{2,1,0:T(2,128)S(1)} all-reduce(f32[1,2,512]{2,1,0:T(2,128)S(1)} %fusion.455), channel_id=5, replica_groups=mesh['pipe'=2,'dp'=64] {'dp'}, use_global_device_ids=true, to_apply=%region_110.111.clone | all-reduce | flops 1024 | bytes 8192
  1506.0 64.6 %all-reduce.1 = f32[512,8]{1,0:T(8,128)S(1)} all-reduce(f32[512,8]{1,0:T(8,128)S(1)} %copy.818), channel_id=6, replica_groups=mesh['pipe'=2,'dp'=64] {'pipe','dp'}, use_global_device_ids=true, to_apply=%region_111.112.clone | all-reduce | flops 4096 | bytes 32768
  1578.7 383.2 %reduce-scatter.14.cloned.1.call-done = f32[64,8]{1,0:T(8,128)} async-done(((f32[8192,8]{1,0:T(8,128)}), f32[64,8]{1,0:T(8,128)}) %reduce-scatter.14.cloned.1.call-update) | async-done | bytes 2064
  1963.9 285.0 %reduce-scatter.10.cloned.1.call-done = f32[1,8,2048]{2,1,0:T(8,128)} async-done(((f32[1,512,2048]{2,1,0:T(8,128)}), f32[1,8,2048]{2,1,0:T(8,128)}) %reduce-scatter.10.cloned.1.call-update) | async-done | bytes 65552 | tf_op jit(solution)/shard_map/reduce_scatter | solution.py:383
  2251.1 287.4 %reduce-scatter.8.cloned.1.call-done = f32[1,8,2048]{2,1,0:T(8,128)} async-done(((f32[1,512,2048]{2,1,0:T(8,128)}), f32[1,8,2048]{2,1,0:T(8,128)}) %reduce-scatter.8.cloned.1.call-update) | async-done | bytes 65552 | tf_op jit(solution)/shard_map/reduce_scatter | solution.py:382
  2540.6 287.4 %reduce-scatter.12.cloned.1.call-done = f32[1,32,512]{2,1,0:T(8,128)} async-done(((f32[1,2048,512]{2,1,0:T(8,128)}), f32[1,32,512]{2,1,0:T(8,128)}) %reduce-scatter.12.cloned.1.call-update) | async-done | bytes 65552 | tf_op jit(solution)/shard_map/reduce_scatter | solution.py:384
  (411 shorter events, 479.6 us)
Async XLA Ops:
  7.2 1954.7 %reduce-scatter.14.cloned.1.call-start = ((), (), s32[]{:S(2)}) async-start(), calls=%async_computation.7 | async-start | bytes 4227072
  68.2 399.7 %collective-permute-start = (bf16[1,1088,512]{2,1,0:T(8,128)(2,1)}, bf16[1,1088,512]{2,1,0:T(8,128)(2,1)S(1)}, u32[]{:S(2)}, u32[]{:S(2)}) collective-permute-start(bf16[1,1088,512]{2,1,0:T(8,128)(2,1)} %get-tuple-element.1110), channel_id=1, source_target_pairs={{0,64},{1,65},{2,66},{3,67},{4,68},{5,69},{6,70},{7,71},{8,72},{9,... | collective-permute-start | bytes 3342344 | tf_op jit(solution)/shard_map/ppermute | solution.py:26
  69.6 401.6 %copy-start.88 = (f32[1,1,512]{2,1,0:T(1,128)}, f32[1,1,512]{2,1,0:T(1,128)S(1)}, u32[]{:S(2)}) copy-start(f32[1,1,512]{2,1,0:T(1,128)S(1)} %get-tuple-element.1920) | copy-start | bytes 6148
  69.6 438.7 %copy-start.79 = (f32[1,1,512]{2,1,0:T(1,128)}, f32[1,1,512]{2,1,0:T(1,128)S(1)}, u32[]{:S(2)}) copy-start(f32[1,1,512]{2,1,0:T(1,128)S(1)} %get-tuple-element.1919) | copy-start | bytes 6148
  91.6 175.6 %copy-start.97 = (bf16[4,8]{1,0:T(4,128)(2,1)S(1)}, bf16[4,8]{1,0:T(4,128)(2,1)}, u32[]{:S(2)}) copy-start(bf16[4,8]{1,0:T(4,128)(2,1)} %param.53) | copy-start | bytes 196
  519.5 36.2 %collective-permute-start.1 = (bf16[1,1088,512]{2,1,0:T(8,128)(2,1)S(1)}, bf16[1,1088,512]{2,1,0:T(8,128)(2,1)S(1)}, u32[]{:S(2)}, u32[]{:S(2)}) collective-permute-start(bf16[1,1088,512]{2,1,0:T(8,128)(2,1)S(1)} %bitcast.955), channel_id=1, source_target_pairs={{0,64},{1,65},{2,66},{3,67},{4,68},{5,69},{6,70},{7,71},{8,72},{9,... | collective-permute-start | bytes 3342344 | tf_op jit(solution)/shard_map/ppermute | solution.py:26
  618.8 312.5 %collective-permute-start.2 = (bf16[1,1088,512]{2,1,0:T(8,128)(2,1)}, bf16[1,1088,512]{2,1,0:T(8,128)(2,1)S(1)}, u32[]{:S(2)}, u32[]{:S(2)}) collective-permute-start(bf16[1,1088,512]{2,1,0:T(8,128)(2,1)} %get-tuple-element.1126), channel_id=1, source_target_pairs={{64,0},{65,1},{66,2},{67,3},{68,4},{69,5},{70,6},{71,7},{72,8},{73... | collective-permute-start | bytes 3342344 | tf_op jit(solution)/shard_map/ppermute | solution.py:26
  622.8 328.4 %copy-start.82 = (f32[1088]{0:T(1024)}, f32[1088]{0:T(1024)S(1)}, u32[]{:S(2)}) copy-start(f32[1088]{0:T(1024)S(1)} %fusion.452) | copy-start | bytes 13060
  622.9 410.7 %copy-start.66 = (f32[1088]{0:T(1024)}, f32[1088]{0:T(1024)S(1)}, u32[]{:S(2)}) copy-start(f32[1088]{0:T(1024)S(1)} %broadcast_multiply_fusion.20) | copy-start | bytes 13060
  1036.8 104.1 %collective-permute-start.3 = (bf16[1,1088,512]{2,1,0:T(8,128)(2,1)}, bf16[1,1088,512]{2,1,0:T(8,128)(2,1)}, u32[]{:S(2)}, u32[]{:S(2)}) collective-permute-start(bf16[1,1088,512]{2,1,0:T(8,128)(2,1)} %bitcast.183), channel_id=1, source_target_pairs={{64,0},{65,1},{66,2},{67,3},{68,4},{69,5},{70,6},{71,7},{72,8},{73... | collective-permute-start | bytes 3342344 | tf_op jit(solution)/shard_map/ppermute | solution.py:26
  1038.1 102.8 %copy-start.34 = (bf16[2,1,1088,512]{3,2,1,0:T(8,128)(2,1)S(1)}, bf16[2,1,1088,512]{3,2,1,0:T(8,128)(2,1)}, u32[]{:S(2)}) copy-start(bf16[2,1,1088,512]{3,2,1,0:T(8,128)(2,1)} %param.45) | copy-start | bytes 6684676
  1038.1 102.8 %copy-start.63 = (bf16[8192,8]{0,1:T(8,128)(2,1)S(1)}, bf16[8192,8]{0,1:T(8,128)(2,1)}, u32[]{:S(2)}) copy-start(bf16[8192,8]{0,1:T(8,128)(2,1)} %reshape.2472) | copy-start | bytes 393220
  1289.7 959.3 %reduce-scatter.10.cloned.1.call-start = ((), (), s32[]{:S(2)}) async-start(), calls=%async_computation.5 | async-start | bytes 4259840 | tf_op jit(solution)/shard_map/reduce_scatter | solution.py:383
  1298.3 1240.2 %reduce-scatter.8.cloned.1.call-start = ((), (), s32[]{:S(2)}) async-start(), calls=%async_computation.4 | async-start | bytes 4259840 | tf_op jit(solution)/shard_map/reduce_scatter | solution.py:382
  1312.8 1515.3 %reduce-scatter.12.cloned.1.call-start = ((), (), s32[]{:S(2)}) async-start(), calls=%async_computation.6 | async-start | bytes 4259840 | tf_op jit(solution)/shard_map/reduce_scatter | solution.py:384
  1331.1 239.6 %copy-start.104 = (f32[1,2,8]{2,1,0:T(2,128)S(1)}, f32[1,2,8]{2,1,0:T(2,128)}, u32[]{:S(2)}) copy-start(f32[1,2,8]{2,1,0:T(2,128)} %param.58) | copy-start | bytes 196
  1331.1 240.8 %copy-start.98 = (bf16[4,8]{1,0:T(4,128)(2,1)S(1)}, bf16[4,8]{1,0:T(4,128)(2,1)}, u32[]{:S(2)}) copy-start(bf16[4,8]{1,0:T(4,128)(2,1)} %param.53) | copy-start | bytes 196
  1331.1 240.8 %copy-start.101 = (f32[4,8]{1,0:T(4,128)S(1)}, f32[4,8]{1,0:T(4,128)}, u32[]{:S(2)}) copy-start(f32[4,8]{1,0:T(4,128)} %param.59) | copy-start | bytes 388
  1575.5 387.2 %copy-start.95 = (bf16[8,64]{1,0:T(8,128)(2,1)S(1)}, bf16[8,64]{1,0:T(8,128)(2,1)}, u32[]{:S(2)}) copy-start(bf16[8,64]{1,0:T(8,128)(2,1)} %param.54) | copy-start | bytes 3076
  1575.5 387.2 %copy-start.99 = (f32[8,64]{1,0:T(8,128)S(1)}, f32[8,64]{1,0:T(8,128)}, u32[]{:S(2)}) copy-start(f32[8,64]{1,0:T(8,128)} %param.60) | copy-start | bytes 6148
  1575.5 673.5 %copy-start.72 = (f32[1,8,2048]{2,1,0:T(8,128)S(1)}, f32[1,8,2048]{2,1,0:T(8,128)}, u32[]{:S(2)}) copy-start(f32[1,8,2048]{2,1,0:T(8,128)} %param.56) | copy-start | bytes 196612
  1575.5 963.0 %copy-start.73 = (f32[1,8,2048]{2,1,0:T(8,128)S(1)}, f32[1,8,2048]{2,1,0:T(8,128)}, u32[]{:S(2)}) copy-start(f32[1,8,2048]{2,1,0:T(8,128)} %param.55) | copy-start | bytes 196612
  1575.5 1252.6 %copy-start.74 = (f32[1,32,512]{2,1,0:T(8,128)S(1)}, f32[1,32,512]{2,1,0:T(8,128)}, u32[]{:S(2)}) copy-start(f32[1,32,512]{2,1,0:T(8,128)} %param.57) | copy-start | bytes 196612
  1962.7 867.5 %copy-start.91 = (f32[8,64]{1,0:T(8,128)}, f32[8,64]{1,0:T(8,128)S(1)}, u32[]{:S(2)}) copy-start(f32[8,64]{1,0:T(8,128)S(1)} %copy.843) | copy-start | bytes 6148
  (81 other events, 671.0 us)
Sparse Core Ops, SparseCore 0:
  1289.8 672.0 reduce-scatter.13
  1964.9 283.9 reduce-scatter.9
  2251.9 286.5 reduce-scatter.7
  2541.4 286.5 reduce-scatter.11
where the time goes:
time: 2850 us; the launch traced here: 2840 us
  waiting for transfers between devices  1660 us (58%)
  blocking collectives  587 us (21%)
  local copies, waits for them, and re-layouts  248 us (9%)
  matrix products  159 us (6%)
  other arithmetic  99.1 us (3%)
  loops' own time  53 us (2%)
    ppermute x4, waiting for transfers between devices, from_behind(): return lax.ppermute(block, axis, route)  415 us
    unnamed x5, waiting for transfers between devices  383 us
    reduce_scatter x1, waiting for transfers between devices, per_device(): lax.psum_scatter(summed[2][None], 'dp', scatter_dimension=1, tiled=True)  287 us
    reduce_scatter x1, waiting for transfers between devices, per_device(): lax.psum_scatter(summed[0][None], 'dp', scatter_dimension=1, tiled=True)  287 us
    reduce_scatter x1, waiting for transfers between devices, per_device(): lax.psum_scatter(summed[1][None], 'dp', scatter_dimension=1, tiled=True)  285 us
    unnamed x2, blocking collectives  235 us
    all_gather x1, blocking collectives, per_device(): lax.all_gather(proj, ('pipe', 'dp'), axis=0, tiled=True)  179 us
    all_gather x1, blocking collectives, per_device(): lax.all_gather(codebook, ('pipe', 'dp'), axis=1, tiled=True)  172 us
  transfers between devices with their start and end apart: 8, of which 7 were waited for; matrix products, arithmetic and copies ran while one was open for 4% of the time, Pallas kernels for 0%

commit v1 on v0

--- a/solution.py
+++ b/solution.py
@@ -1,6 +1,8 @@
 import jax
 import jax.numpy as jnp
 from jax import lax
+from jax.experimental import pallas as pl
+from jax.experimental.pallas import tpu as pltpu
 from jax.sharding import PartitionSpec as P
 
 D = 512
@@ -9,6 +11,8 @@
 FF = 2048
 CODES = 8192
 CODE_DIM = 8
+ROWS_OF_CODES = 128
+LOW_CODES = 64
 PATCHES = 64
 FRAMES = 17
 SEQ = 1088
@@ -18,6 +22,182 @@
 BETA = 0.25
 LEARN_RATE = 0.0001
 MASKED = -1e30
+MESH = pl.DeviceIdType.MESH
+WIDE = 3200
+
+
+def gather_kernel(block_ref, out_ref, landed, send_sems, recv_sems):
+    pipe = lax.axis_index("pipe")
+    dp = lax.axis_index("dp")
+    own = pipe * 64 + dp
+
+    def copy_to(step):
+        target = lax.rem(dp + step, 64)
+        return pltpu.make_async_remote_copy(
+            src_ref=block_ref,
+            dst_ref=landed.at[own],
+            send_sem=send_sems.at[step],
+            recv_sem=recv_sems.at[own],
+            device_id=(1, target),
+            device_id_type=MESH,
+        )
+
+    def start(step, carry):
+        copy_to(step).start()
+        return carry
+
+    def finish(step, carry):
+        copy_to(step).wait_send()
+        return carry
+
+    @pl.when(pipe == 0)
+    def _():
+        copy_to(0).start()
+
+    lax.fori_loop(1, 64, start, 0)
+
+    @pl.when(pipe == 0)
+    def _():
+        copy_to(0).wait_send()
+        out_ref[...] = jnp.zeros_like(out_ref)
+
+    lax.fori_loop(1, 64, finish, 0)
+
+    @pl.when(pipe == 1)
+    def _():
+        landed[own] = block_ref[...]
+
+        def arrive(step, carry):
+            source = lax.rem(own + step, 128)
+            pltpu.make_async_remote_copy(
+                src_ref=block_ref,
+                dst_ref=landed.at[source],
+                send_sem=send_sems.at[0],
+                recv_sem=recv_sems.at[source],
+                device_id=(1, lax.rem(dp + 1, 64)),
+                device_id_type=MESH,
+            ).wait_recv()
+            return carry
+
+        lax.fori_loop(1, 128, arrive, 0)
+        out_ref[...] = landed[...]
+
+
+def gather_blocks(block):
+    return pl.pallas_call(
+        gather_kernel,
+        out_shape=jax.ShapeDtypeStruct((128, 8, 128), jnp.float32),
+        in_specs=[pl.BlockSpec(memory_space=pltpu.VMEM)],
+        out_specs=pl.BlockSpec(memory_space=pltpu.VMEM),
+        scratch_shapes=[
+            pltpu.VMEM((128, 8, 128), jnp.float32),
+            pltpu.SemaphoreType.DMA((64,)),
+            pltpu.SemaphoreType.DMA((128,)),
+        ],
+        compiler_params=pltpu.CompilerParams(has_side_effects=True),
+    )(block)
+
+
+def chip_after(chip, step):
+    x = lax.rem(lax.rem(chip, 4) + lax.rem(step, 4), 4)
+    z = lax.rem(lax.rem(chip // 4, 2) + lax.rem(step // 4, 2), 2)
+    y = lax.rem(chip // 8 + step // 8, 4)
+    return (y * 2 + z) * 4 + x
+
+
+def scatter_kernel(blocks, out_ref, mine, other, landed, local_sems, near_send, near_recv, far_send, far_recv):
+    pipe = lax.axis_index("pipe")
+    dp = lax.axis_index("dp")
+    core = lax.rem(dp, 2)
+    chip = dp // 2
+    partner = dp + 1 - 2 * core
+
+    def near(step):
+        target = chip_after(chip, step)
+        return pltpu.make_async_remote_copy(
+            src_ref=blocks.at[1 - core, target],
+            dst_ref=other.at[target],
+            send_sem=near_send.at[step],
+            recv_sem=near_recv.at[step],
+            device_id=(pipe, partner),
+            device_id_type=MESH,
+        )
+
+    def local(step):
+        target = chip_after(chip, step)
+        return pltpu.make_async_copy(blocks.at[core, target], mine.at[target], local_sems.at[step])
+
+    def far(step):
+        target = chip_after(chip, step)
+        return pltpu.make_async_remote_copy(
+            src_ref=mine.at[target],
+            dst_ref=landed.at[step],
+            send_sem=far_send.at[step],
+            recv_sem=far_recv.at[step],
+            device_id=(pipe, target * 2 + core),
+            device_id_type=MESH,
+        )
+
+    def begin(step, carry):
+        at = lax.rem(step + 1, 32)
+        near(at).start()
+        local(at).start()
+        return carry
+
+    lax.fori_loop(0, 32, begin, 0)
+
+    def pair(step, carry):
+        target = chip_after(chip, step)
+        local(step).wait()
+        near(step).wait_recv()
+        mine[target] = (mine[target].astype(jnp.float32) + other[target].astype(jnp.float32)).astype(jnp.bfloat16)
+        far(step).start()
+        return carry
+
+    lax.fori_loop(1, 32, pair, 0)
+    local(0).wait()
+    near(0).wait_recv()
+    out_ref[...] = mine[chip].astype(jnp.float32) + other[chip].astype(jnp.float32)
+
+    def total(step, carry):
+        far(step).wait_recv()
+        out_ref[...] += landed[step].astype(jnp.float32)
+        return carry
+
+    lax.fori_loop(1, 32, total, 0)
+
+    def finish(step, carry):
+        near(step).wait_send()
+        return carry
+
+    lax.fori_loop(0, 32, finish, 0)
+
+    def finish_far(step, carry):
+        far(step).wait_send()
+        return carry
+
+    lax.fori_loop(1, 32, finish_far, 0)
+
+
+def scatter_blocks(blocks):
+    shape = (32, 16, WIDE)
+    return pl.pallas_call(
+        scatter_kernel,
+        out_shape=jax.ShapeDtypeStruct((16, WIDE), jnp.float32),
+        in_specs=[pl.BlockSpec(memory_space=pl.ANY)],
+        out_specs=pl.BlockSpec(memory_space=pltpu.VMEM),
+        scratch_shapes=[
+            pltpu.VMEM(shape, jnp.bfloat16),
+            pltpu.VMEM(shape, jnp.bfloat16),
+            pltpu.VMEM(shape, jnp.bfloat16),
+            pltpu.SemaphoreType.DMA((32,)),
+            pltpu.SemaphoreType.DMA((32,)),
+            pltpu.SemaphoreType.DMA((32,)),
+            pltpu.SemaphoreType.DMA((32,)),
+            pltpu.SemaphoreType.DMA((32,)),
+        ],
+        compiler_params=pltpu.CompilerParams(has_side_effects=True, vmem_limit_bytes=40 << 20),
+    )(blocks)
 
 
 def from_behind(block, axis, distance):
@@ -230,6 +410,55 @@
 
 def average(ema, weight, grad, rate):
     return rate * ema + (1.0 - rate) * (weight - LEARN_RATE * grad)
+
+
+def gather_quant(proj, codebook):
+    flat = jnp.concatenate([codebook.reshape(512), proj.reshape(32), jnp.zeros((480,), proj.dtype)])
+    parts = gather_blocks(flat.astype(jnp.float32).reshape(8, 128)).reshape(128, 1024)
+    parts = parts.astype(jnp.bfloat16)
+    return (parts[:, 512:544].reshape(D, CODE_DIM), parts[:, :512])
+
+
+def reduce_shards(grads, quant_grads):
+    attn, up, down, gain = grads
+    grad_proj, grad_code = quant_grads
+    wide = [
+        jnp.swapaxes(w.reshape(64, 8, 2, 1024), 1, 2).reshape(64, 16, 1024) for w in (attn, up)
+    ]
+    tall = jnp.swapaxes(down.reshape(64, 2, 16, 512), 1, 2).reshape(64, 16, 1024)
+    few = jnp.concatenate(
+        [
+            grad_code[:64],
+            grad_code[64:],
+            jnp.swapaxes(gain.reshape(2, 64, 8), 0, 1).reshape(64, 16),
+            grad_proj[:256].reshape(64, 32),
+            grad_proj[256:].reshape(64, 32),
+            jnp.zeros((64, 944), jnp.float32),
+        ],
+        axis=1,
+    ).reshape(64, 16, 128)
+    blocks = jnp.concatenate([wide[0], wide[1], tall, few], axis=2).astype(jnp.bfloat16)
+    blocks = jnp.swapaxes(blocks.reshape(32, 2, 16, WIDE), 0, 1)
+    total = scatter_blocks(blocks)
+    rows = [
+        jnp.swapaxes(total[:, i : i + 1024].reshape(2, 8, 1024), 0, 1).reshape(1, 8, 2048)
+        for i in (0, 1024)
+    ]
+    down_rows = jnp.swapaxes(total[:, 2048:3072].reshape(16, 2, 512), 0, 1).reshape(1, 32, 512)
+    few = total[:, 3072:].reshape(2048)
+    gain_part = few[1024:1040].reshape(1, 2, 8)
+    first_quant = jnp.concatenate([few[:512], few[1040:1072], jnp.zeros((480,), jnp.float32)])
+    first_quant = lax.ppermute(first_quant.reshape(8, 128), "pipe", [(1, 0)]).reshape(1024)
+    second_quant = jnp.concatenate([few[512:1024], few[1072:1104], jnp.zeros((480,), jnp.float32)])
+    quant = jnp.where(lax.axis_index("pipe") == 0, first_quant, second_quant)
+    return (
+        rows[0],
+        rows[1],
+        down_rows,
+        gain_part,
+        quant[512:544].reshape(4, CODE_DIM),
+        quant[:512].reshape(CODE_DIM, LOW_CODES),
+    )
 
 
 def per_device(
@@ -257,10 +486,7 @@
     micro = video.shape[0]
     videos = video.shape[1]
     weights = (w_attn[0], w_up[0], w_down[0], gains[0])
-    proj_all, code_all = (
-        lax.all_gather(proj, ("pipe", "dp"), axis=0, tiled=True),
-        lax.all_gather(codebook, ("pipe", "dp"), axis=1, tiled=True),
-    )
+    proj_all, code_table = gather_quant(proj, codebook)
     slots = micro + 2
     row_count = videos * SEQ
 
@@ -277,7 +503,7 @@
         return jax.tree.map(lambda w: jnp.zeros(w.shape, jnp.float32), weights)
 
     def empty_quant():
-        return (jnp.zeros((D, CODE_DIM), jnp.float32), jnp.zeros((CODE_DIM, CODES), jnp.float32))
+        return (jnp.zeros((D, CODE_DIM), jnp.float32), jnp.zeros((ROWS_OF_CODES, CODE_DIM * LOW_CODES), jnp.float32))
 
     def run_forward(inputs, frame_count):
         return block_forward(weights, inputs, frame_count, first)
@@ -314,17 +540,17 @@
         rows = out_low.reshape(-1, D)
         mask = valid.reshape(-1, 1)
         latent = jnp.dot(rows, proj_all, preferred_element_type=jnp.float32)
-        onehot_cols = (jnp.arange(CODES)[:, None] == code_now.reshape(-1)[None, :]).astype(
-            jnp.bfloat16
-        )
-        chosen = jnp.dot(code_all, onehot_cols, preferred_element_type=jnp.float32).T
+        code = code_now.reshape(-1, 1)
+        high = (code // LOW_CODES == jnp.arange(ROWS_OF_CODES)[None, :]).astype(jnp.bfloat16)
+        low = (code % LOW_CODES == jnp.arange(LOW_CODES)[None, :])[:, None, :]
+        near = jnp.dot(high, code_table, preferred_element_type=jnp.float32)
+        chosen = jnp.sum(jnp.where(low, near.reshape(-1, CODE_DIM, LOW_CODES), 0.0), axis=2)
         cot_codes = jnp.swapaxes(cot_q_now, 1, 2).reshape(-1, CODE_DIM).astype(jnp.float32)
         d_latent = (cot_codes * mask + 2.0 * BETA * mask * (latent - chosen)).astype(jnp.bfloat16)
         d_chosen = (2.0 * mask * (chosen - latent)).astype(jnp.bfloat16)
         grad_proj = jnp.dot(rows.T, d_latent, preferred_element_type=jnp.float32)
-        grad_code = lax.dot_general(
-            d_chosen.T, onehot_cols, (((1,), (1,)), ((), ())), preferred_element_type=jnp.float32
-        )
+        spread = jnp.where(low, d_chosen[:, :, None], 0).reshape(-1, CODE_DIM * LOW_CODES)
+        grad_code = jnp.dot(high.T, spread, preferred_element_type=jnp.float32)
         d_rows = jnp.dot(d_latent, proj_all.T, preferred_element_type=jnp.float32)
         d_out = cot_h_now.reshape(-1, D).astype(jnp.float32) * mask + d_rows
         return (d_out, (grad_proj, grad_code))
@@ -343,7 +569,6 @@
         return (jnp.zeros_like(inputs), empty_grads(), empty_quant())
 
     summed = empty_grads()
-    shards = None
     quant_summed = empty_quant()
     store_back = jnp.zeros((slots,) + video.shape[1:], jnp.bfloat16)
     returned = jnp.zeros_like(video[0])
@@ -378,17 +603,7 @@
         if tick < micro:
             returned = from_behind(d_input, "pipe", -1)
         summed = jax.tree.map(lambda a, b: a + b, summed, grads)
-    shards = (
-        lax.psum_scatter(summed[0][None], "dp", scatter_dimension=1, tiled=True),
-        lax.psum_scatter(summed[1][None], "dp", scatter_dimension=1, tiled=True),
-        lax.psum_scatter(summed[2][None], "dp", scatter_dimension=1, tiled=True),
-        lax.psum_scatter(summed[3][None], "dp", scatter_dimension=2, tiled=True),
-    )
-    g_attn, g_up, g_down, g_gains = shards
-    g_proj, g_code = (
-        lax.psum_scatter(quant_summed[0], ("pipe", "dp"), scatter_dimension=0, tiled=True),
-        lax.psum_scatter(quant_summed[1], ("pipe", "dp"), scatter_dimension=1, tiled=True),
-    )
+    g_attn, g_up, g_down, g_gains, g_proj, g_code = reduce_shards(summed, quant_summed)
     valid_all = (jnp.arange(SEQ)[None, None, :] // PATCHES < frames[:, :, None]).astype(
         jnp.float32
     )[..., None]

time: 2850 us -> 1100 us (0.39)
  waiting for transfers between devices: 1660 us -> 395 us
  blocking collectives: 587 us -> 0 us
  Pallas kernels: 0 us -> 78.1 us
  starting transfers between devices: 16.1 us -> 58.9 us
    reduce_scatter x3 -> x0, waiting for transfers between devices: 860 us -> none  [the longest x1 287 us: per_device(): lax.psum_scatter(summed[2][None], 'dp', scatter_dimension=1, tiled=True)]
    unnamed x5 -> x0, waiting for transfers between devices: 383 us -> none
    all_gather x2 -> x0, blocking collectives: 351 us -> none  [the longest x1 179 us: per_device(): lax.all_gather(proj, ('pipe', 'dp'), axis=0, tiled=True)]
    unnamed x2 -> x0, blocking collectives: 235 us -> none
    pallas_call x0 -> x2, Pallas kernels: none -> 78.1 us  [the longest x1 64.1 us: scatter_blocks(): pl.pallas_call(scatter_kernel, out_shape=jax.ShapeDtypeStruct((16, WIDE),...]
    ppermute x4, starting transfers between devices: 16 us -> 57.6 us  [from_behind(): return lax.ppermute(block, axis, route)]
  transfers between devices with their start and end apart: 8 -> 5, of which waited for: 7 -> 3; matrix products, arithmetic and copies ran while one was open for 4% -> 9% of each run, Pallas kernels for 0% -> 1%
where the time goes in v1:
time: 1100 us; the launch traced here: 1090 us
  waiting for transfers between devices  395 us (36%)
  local copies, waits for them, and re-layouts  253 us (23%)
  matrix products  162 us (15%)
  other arithmetic  94.6 us (9%)
  Pallas kernels  78.1 us (7%)
  starting transfers between devices  58.9 us (5%)
  loops' own time  41.2 us (4%)
    ppermute x4, waiting for transfers between devices, from_behind(): return lax.ppermute(block, axis, route)  395 us
    pallas_call x1, Pallas kernels, scatter_blocks(): pl.pallas_call(scatter_kernel, out_shape=jax.ShapeDtypeStruct((16, WIDE),...  64.1 us
    ppermute x4, starting transfers between devices, from_behind(): return lax.ppermute(block, axis, route)  57.6 us
    reshape x8, local copies, waits for them, and re-layouts, spatial_groups(): tokens.reshape((tokens.shape[0] * FRAMES, PATCHES) + tokens.shape[2:])  45.3 us
    dynamic_update_slice x13, local copies, waits for them, and re-layouts, per_device(): lax.dynamic_update_index_in_dim(buffer, value, which, 0)  39.2 us
    broadcast_in_dim x4, local copies, waits for them, and re-layouts, per_device(): jnp.zeros((slots,) + a.shape, a.dtype)  23 us
  transfers between devices with their start and end apart: 5, of which 3 were waited for; matrix products, arithmetic and copies ran while one was open for 9% of the time, Pallas kernels for 1%

profile of v1, /device:TPU:0, one launch (start us, length us, event | category | flops | bytes accessed | tf_op | source)
XLA Modules:
  0.0 1086.1 jit_solution(5619739137029188959)
XLA Ops:
  4.7 57.3 %conditional.13 = (bf16[1,1088,512]{2,1,0:T(8,128)(2,1)}, bf16[1,1,1088,512]{3,2,1,0:T(8,128)(2,1)}, bf16[1,1,1088,1536]{3,2,1,0:T(8,128)(2,1)}, bf16[1,1,1088,5...) conditional(s32[]{:T(128)} %convert_element_type.1000, ...), branch_computations={%region_0.1_spmd, %region_1.14_spmd} | conditional | flops 7029483008 | bytes 135512096 | solution.py:524
  11.1 29.6 %conditional = (bf16[1088,512]{1,0:T(8,128)(2,1)}, bf16[1,1,1088,512]{3,2,1,0:T(8,128)(2,1)}, f32[1,1,1088,8]{2,3,1,0:T(8,128)S(1)}) conditional(s32[]{:T(128)} %convert_element_type.841, (s32[]{:T(128)}, s32[2,1]{0,1:T(1,128)S(1)}, bf16[1088,1536]{1,0:T(8,128)(2,1)}) %tuple.167, bf16[1088,1536]{1,0:T(8,128)(2,1)} %convolution_convert_fusion), branch_computations={%region_4.8_spmd, %region_9.11_spmd} | conditional | flops 147611136 | bytes 50797808 | solution.py:352
  92.9 14.0 %shard_map.281 = f32[128,8,128]{2,1,0:T(8,128)} custom-call(f32[8,128]{1,0:T(8,128)} %fusion.466.block_ref), custom_call_target="tpu_custom_call" | custom-call | tf_op jit(solution)/shard_map/pallas_call | solution.py:87
  112.0 11.9 %broadcast_in_dim.562 = f32[4,1088,2048]{2,1,0:T(8,128)} broadcast(f32[]{:T(128)} %constant.940.clone.1), dimensions={} | broadcast | bytes 35651588 | tf_op jit(solution)/shard_map/broadcast_in_dim | solution.py:516
  140.5 29.5 %conditional.14 = (bf16[1088,512]{1,0:T(8,128)(2,1)}, bf16[1,1,1088,512]{3,2,1,0:T(8,128)(2,1)}, f32[1,1,1088,8]{2,3,1,0:T(8,128)S(1)}) conditional(s32[]{:T(128)} %convert_element_type.1000, (s32[]{:T(128)}, s32[2,1]{0,1:T(1,128)S(1)}, bf16[1088,1536]{1,0:T(8,128)(2,1)}) %tuple.403, bf16[1088,1536]{1,0:T(8,128)(2,1)} %get-tuple-element.1731), branch_computations={%region_16.21_spmd, %region_21.24_spmd} | conditional | flops 147611136 | bytes 50797792 | solution.py:352
  146.7 9.3 reshape.2878
  184.0 53.5 %collective-permute-start.1 = (bf16[1,1088,512]{2,1,0:T(8,128)(2,1)S(1)}, bf16[1,1088,512]{2,1,0:T(8,128)(2,1)S(1)}, u32[]{:S(2)}, u32[]{:S(2)}) collective-permute-start(bf16[1,1088,512]{2,1,0:T(8,128)(2,1)S(1)} %bitcast.1015), channel_id=1, source_target_pairs={{0,64},{1,65},{2,66},{3,67},{4,68},{5,69},{6,70},{7,71},{8,72},{9,... | collective-permute-start | bytes 3342344 | tf_op jit(solution)/shard_map/ppermute | solution.py:206
  240.8 20.7 %collective-permute-done.1 = bf16[1,1088,512]{2,1,0:T(8,128)(2,1)S(1)} collective-permute-done((bf16[1,1088,512]{2,1,0:T(8,128)(2,1)S(1)}, bf16[1,1088,512]{2,1,0:T(8,128)(2,1)S(1)}, u32[]{:S(2)}, u32[]{:S(2)}) %collective-permute-start.1) | collective-permute-done | bytes 1114144 | tf_op jit(solution)/shard_map/ppermute | solution.py:206
  262.9 15.3 %conditional.15 = (bf16[1,1,1088,512]{3,2,1,0:T(8,128)(2,1)}, bf16[1,1,1088,1536]{3,2,1,0:T(8,128)(2,1)}, bf16[1,1,1088,512]{3,2,1,0:T(8,128)(2,1)}, f32[1,1,108...) conditional(s32[]{:T(128)} %convert_element_type.1008, () %tuple.210, ...), branch_computations={%region_26.27_spmd, %region_27.40_spmd} | conditional | flops 7027254784 | bytes 127778792 | solution.py:524
  307.2 15.2 %conditional.16 = (bf16[1,1088,512]{2,1,0:T(8,128)(2,1)}, f32[512,2048]{1,0:T(8,128)}, f32[512,2048]{1,0:T(8,128)}, f32[2048,512]{1,0:T(8,128)}, f32[2,512]{1,0:...) conditional(s32[]{:T(128)} %convert_element_type.1008, () %tuple.212, ...), branch_computations={%region_40.41_spmd, %region_41.64_spmd} | conditional | flops 14475629568 | bytes 327725312 | solution.py:588
  334.4 294.8 %collective-permute-done.2 = bf16[1,1088,512]{2,1,0:T(8,128)(2,1)S(1)} collective-permute-done((bf16[1,1088,512]{2,1,0:T(8,128)(2,1)}, bf16[1,1088,512]{2,1,0:T(8,128)(2,1)S(1)}, u32[]{:S(2)}, u32[]{:S(2)}) %collective-permute-start.2) | collective-permute-done | bytes 1114144 | tf_op jit(solution)/shard_map/ppermute | solution.py:206
  632.2 10.2 fusion.378
  661.3 66.9 %conditional.18 = (bf16[1,1088,1536]{2,1,0:T(8,128)(2,1)}) conditional(s32[]{:T(128)} %convert_element_type.1000, (s32[1,1]{1,0:T(1,128)}, bf16[1,1088,1536]{2,1,0:T(8,128)(2,1)}, f32[1,1088,8]{1,2,0:T(8,128)S(1)}, bf16[1088,512]{1,0:T(8,128)(2,1)}) %tuple.382, (bf16[1,1088,1536]{2,1,0:T(8,128)(2,1)}, f32[1,1088,8]{1,2,0:T(8,128)S(1)}, ...), branch_computations={%region_71.78_spmd, %region_78.80_spmd} | conditional | flops 368762368 | bytes 118131648 | solution.py:389
  708.3 10.2 copy.541
  718.5 9.6 reshape.2911
  749.1 9.8 fusion.392
  759.0 79.6 %collective-permute-done.3 = bf16[1,1088,512]{2,1,0:T(8,128)(2,1)S(1)} collective-permute-done((bf16[1,1088,512]{2,1,0:T(8,128)(2,1)S(1)}, bf16[1,1088,512]{2,1,0:T(8,128)(2,1)S(1)}, u32[]{:S(2)}, u32[]{:S(2)}) %collective-permute-start.3) | collective-permute-done | bytes 1114144 | tf_op jit(solution)/shard_map/ppermute | solution.py:206
  838.6 138.9 %conditional.19 = (f32[512,2048]{1,0:T(8,128)}, f32[512,2048]{1,0:T(8,128)}, f32[2048,512]{1,0:T(8,128)}, f32[2,512]{1,0:T(2,128)S(1)}, f32[512,8]{0,1:T(8,128)}...) conditional(s32[]{:T(128)} %convert_element_type.1000, () %tuple.217, ...), branch_computations={%region_84.85_spmd, %region_85.108_spmd} | conditional | flops 14475629568 | bytes 325437536 | solution.py:588
  847.5 10.2 fusion.319
  875.9 66.8 %conditional.5 = (bf16[1,1088,1536]{2,1,0:T(8,128)(2,1)}) conditional(s32[]{:T(128)} %convert_element_type.956, (s32[1,1]{1,0:T(1,128)}, bf16[1,1088,1536]{2,1,0:T(8,128)(2,1)}, f32[1,1088,8]{1,2,0:T(8,128)S(1)}, bf16[1088,512]{1,0:T(8,128)(2,1)}) %tuple.190, (bf16[1,1088,1536]{2,1,0:T(8,128)(2,1)}, f32[1,1088,8]{1,2,0:T(8,128)S(1)}, ...), branch_computations={%region_95.101_spmd, %region_102.103_spmd} | conditional | flops 368762368 | bytes 118131648 | solution.py:389
  922.7 10.2 copy.557
  932.9 9.6 reshape.2923
  967.6 9.7 fusion.323
  1003.2 64.1 %shard_map.282 = f32[16,3200]{1,0:T(8,128)S(1)} custom-call(bf16[2,32,16,3200]{3,2,1,0:T(8,128)(2,1)S(1)} %copy_bitcast_fusion.48.blocks), custom_call_target="tpu_custom_call" | custom-call | tf_op jit(solution)/shard_map/pallas_call | solution.py:184
  (428 shorter events, 419.2 us)
Async XLA Ops:
  3.0 60.5 %copy-start.97 = (bf16[8,64]{1,0:T(8,128)(2,1)S(1)}, bf16[8,64]{1,0:T(8,128)(2,1)}, u32[]{:S(2)}) copy-start(bf16[8,64]{1,0:T(8,128)(2,1)} %param.54) | copy-start | bytes 3076
  3.0 60.5 %copy-start.105 = (bf16[4,8]{1,0:T(4,128)(2,1)S(1)}, bf16[4,8]{1,0:T(4,128)(2,1)}, u32[]{:S(2)}) copy-start(bf16[4,8]{1,0:T(4,128)(2,1)} %param.53) | copy-start | bytes 196
  62.0 70.3 %collective-permute-start = (bf16[1,1088,512]{2,1,0:T(8,128)(2,1)}, bf16[1,1088,512]{2,1,0:T(8,128)(2,1)S(1)}, u32[]{:S(2)}, u32[]{:S(2)}) collective-permute-start(bf16[1,1088,512]{2,1,0:T(8,128)(2,1)} %get-tuple-element.1110), channel_id=1, source_target_pairs={{0,64},{1,65},{2,66},{3,67},{4,68},{5,69},{6,70},{7,71},{8,72},{9,... | collective-permute-start | bytes 3342344 | tf_op jit(solution)/shard_map/ppermute | solution.py:206
  63.4 72.2 %copy-start.92 = (f32[1,1,512]{2,1,0:T(1,128)}, f32[1,1,512]{2,1,0:T(1,128)S(1)}, u32[]{:S(2)}) copy-start(f32[1,1,512]{2,1,0:T(1,128)S(1)} %get-tuple-element.1723) | copy-start | bytes 6148
  63.4 109.3 %copy-start.82 = (f32[1,1,512]{2,1,0:T(1,128)}, f32[1,1,512]{2,1,0:T(1,128)S(1)}, u32[]{:S(2)}) copy-start(f32[1,1,512]{2,1,0:T(1,128)S(1)} %get-tuple-element.1722) | copy-start | bytes 6148
  179.9 58.2 %copy-start.33 = (bf16[1,1,1088,512]{3,2,1,0:T(8,128)(2,1)S(1)}, bf16[1,1,1088,512]{3,2,1,0:T(8,128)(2,1)}, u32[]{:S(2)}) copy-start(bf16[1,1,1088,512]{3,2,1,0:T(8,128)(2,1)} %get-tuple-element.1123) | copy-start | bytes 3342340
  184.0 77.6 %collective-permute-start.1 = (bf16[1,1088,512]{2,1,0:T(8,128)(2,1)S(1)}, bf16[1,1088,512]{2,1,0:T(8,128)(2,1)S(1)}, u32[]{:S(2)}, u32[]{:S(2)}) collective-permute-start(bf16[1,1088,512]{2,1,0:T(8,128)(2,1)S(1)} %bitcast.1015), channel_id=1, source_target_pairs={{0,64},{1,65},{2,66},{3,67},{4,68},{5,69},{6,70},{7,71},{8,72},{9,... | collective-permute-start | bytes 3342344 | tf_op jit(solution)/shard_map/ppermute | solution.py:206
  239.2 22.3 %copy-start.28 = (bf16[2,1,1088,512]{3,2,1,0:T(8,128)(2,1)S(1)}, bf16[2,1,1088,512]{3,2,1,0:T(8,128)(2,1)}, u32[]{:S(2)}) copy-start(bf16[2,1,1088,512]{3,2,1,0:T(8,128)(2,1)} %param.44) | copy-start | bytes 6684676
  307.2 16.6 %copy-start.84 = (f32[1088]{0:T(1024)S(1)}, f32[1088]{0:T(1024)}, u32[]{:S(2)}) copy-start(f32[1088]{0:T(1024)} %dynamic-slice_reduce_fusion.5) | copy-start | bytes 13060
  322.5 306.7 %collective-permute-start.2 = (bf16[1,1088,512]{2,1,0:T(8,128)(2,1)}, bf16[1,1088,512]{2,1,0:T(8,128)(2,1)S(1)}, u32[]{:S(2)}, u32[]{:S(2)}) collective-permute-start(bf16[1,1088,512]{2,1,0:T(8,128)(2,1)} %get-tuple-element.1126), channel_id=1, source_target_pairs={{64,0},{65,1},{66,2},{67,3},{68,4},{69,5},{70,6},{71,7},{72,8},{73... | collective-permute-start | bytes 3342344 | tf_op jit(solution)/shard_map/ppermute | solution.py:206
  632.2 10.2 copy-start.83
  661.3 66.9 %copy-start.93 = (f32[1,1,512]{2,1,0:T(1,128)S(1)}, f32[1,1,512]{2,1,0:T(1,128)}, u32[]{:S(2)}) copy-start(f32[1,1,512]{2,1,0:T(1,128)} %copy-done.92) | copy-start | bytes 6148
  744.6 94.0 %collective-permute-start.3 = (bf16[1,1088,512]{2,1,0:T(8,128)(2,1)S(1)}, bf16[1,1088,512]{2,1,0:T(8,128)(2,1)S(1)}, u32[]{:S(2)}, u32[]{:S(2)}) collective-permute-start(bf16[1,1088,512]{2,1,0:T(8,128)(2,1)S(1)} %bitcast.946), channel_id=1, source_target_pairs={{64,0},{65,1},{66,2},{67,3},{68,4},{69,5},{70,6},{71,7},{72,8},{73... | collective-permute-start | bytes 3342344 | tf_op jit(solution)/shard_map/ppermute | solution.py:206
  749.1 89.5 %copy-start.31 = (bf16[2,1,1088,512]{3,2,1,0:T(8,128)(2,1)S(1)}, bf16[2,1,1088,512]{3,2,1,0:T(8,128)(2,1)}, u32[]{:S(2)}) copy-start(bf16[2,1,1088,512]{3,2,1,0:T(8,128)(2,1)} %param.45) | copy-start | bytes 6684676
  749.1 89.5 %copy-start.69 = (bf16[128,512]{1,0:T(8,128)(2,1)S(1)}, bf16[128,512]{1,0:T(8,128)(2,1)}, u32[]{:S(2)}) copy-start(bf16[128,512]{1,0:T(8,128)(2,1)} %slice.382) | copy-start | bytes 393220
  749.1 89.5 %copy-start.90 = (s32[2,1,1088]{2,1,0:T(1,128)S(1)}, s32[2,1,1088]{2,1,0:T(1,128)}, u32[]{:S(2)}) copy-start(s32[2,1,1088]{2,1,0:T(1,128)} %param.48) | copy-start | bytes 26116
  749.1 89.5 %copy-start.113 = (s32[2,1]{0,1:T(1,128)S(1)}, s32[2,1]{0,1:T(1,128)}, u32[]{:S(2)}) copy-start(s32[2,1]{0,1:T(1,128)} %param.47) | copy-start | bytes 28
  847.5 10.2 copy-start.55
  847.5 10.3 copy-start.45
  1067.5 15.6 %collective-permute-start.4 = (f32[8,128]{1,0:T(8,128)S(1)}, f32[8,128]{1,0:T(8,128)S(1)}, u32[]{:S(2)}, u32[]{:S(2)}) collective-permute-start(f32[8,128]{1,0:T(8,128)S(1)} %get-tuple-element.1724), channel_id=1, source_target_pairs={{64,0},{65,1},{66,2},{67,3},{68,4},{69,5},{70,6},{71,7},{72,8},{73... | collective-permute-start | bytes 12296 | tf_op jit(solution)/shard_map/ppermute | solution.py:451
  1071.3 11.9 %copy-start.98 = (bf16[8,64]{1,0:T(8,128)(2,1)S(1)}, bf16[8,64]{1,0:T(8,128)(2,1)}, u32[]{:S(2)}) copy-start(bf16[8,64]{1,0:T(8,128)(2,1)} %param.54) | copy-start | bytes 3076
  1071.3 11.9 %copy-start.100 = (f32[8,64]{1,0:T(8,128)S(1)}, f32[8,64]{1,0:T(8,128)}, u32[]{:S(2)}) copy-start(f32[8,64]{1,0:T(8,128)} %param.60) | copy-start | bytes 6148
  1071.3 13.1 %copy-start.101 = (f32[4,8]{1,0:T(4,128)S(1)}, f32[4,8]{1,0:T(4,128)}, u32[]{:S(2)}) copy-start(f32[4,8]{1,0:T(4,128)} %param.59) | copy-start | bytes 388
  1071.4 13.1 %copy-start.106 = (bf16[4,8]{1,0:T(4,128)(2,1)S(1)}, bf16[4,8]{1,0:T(4,128)(2,1)}, u32[]{:S(2)}) copy-start(bf16[4,8]{1,0:T(4,128)(2,1)} %param.53) | copy-start | bytes 196
  (76 other events, 351.0 us)
